TPU v7x, 32 devices: a whole 2x2x4 slice. The times are simulated.
32 devices in a mesh: grp: 2 (over y), exp: 4 (over z), rep: 4 (over x, core).
Axes of the slice: x: 2, y: 2, z: 4, core: 2. Of those that a mesh axis runs over, the one named last changes fastest.
Arguments:
- tokens: bfloat16 [4096, 1024], P(('grp', 'exp', 'rep')), parts along dimension 0, may hold values from -6 to 6
- routes: int32 [4096, 2], P(('grp', 'exp', 'rep')), parts along dimension 0, may hold values from 0 to 7, all different within a row; in each aligned block of 128 rows (0 to 127, 128 to 255, ...) at most 48 rows name the same one
- combine: float32 [4096, 2], P(('grp', 'exp', 'rep')), parts along dimension 0, may hold values from 0.2 to 1
- w_gate: bfloat16 [8, 1024, 2048], P('exp', None, 'rep'), may hold values from -0.1875 to 0.1875
- w_up: bfloat16 [8, 1024, 2048], P('exp', None, 'rep'), may hold values from -0.1875 to 0.1875
- w_down: bfloat16 [8, 2048, 1024], P('exp', 'rep'), may hold values from -0.125 to 0.125
Outputs:
- expert_mix: bfloat16 [4096, 1024], P(('grp', 'exp', 'rep')), parts along dimension 0
There are 2 independent parts, one for each index of `grp`. A program takes and returns all parts, laid end to end along the dimension named above; an argument that names none is the same for every part. Nothing has to cross between parts.
Inputs may be any that keep to these rules, and one draw needn't show every extreme that they name: `routes`: each row names 2 different experts. Within the 128 tokens of one device no expert is named more than 48 times, a bound that some block reaches.
All inputs are finite; a program needn't handle non-finite values.
Results may differ from a plain program's by a relative error of at most 0.0078.
Values may be sent and summed in bfloat16 or wider, within the bound.
A program may use at most 64 MiB of HBM per device.

v0:
```python
import jax
import jax.numpy as jnp
from jax import lax
from jax.sharding import PartitionSpec as P


def rms_rows(tokens):
    values = tokens.astype(jnp.float32)
    scale = lax.rsqrt(jnp.mean(values * values, axis=-1, keepdims=True) + 1e-05)
    return (values * scale).astype(jnp.bfloat16)


def slot_numbers(routes, experts, capacity):
    flat = routes.reshape(-1)
    onehot = (flat[:, None] == jnp.arange(experts, dtype=jnp.int32)[None, :]).astype(jnp.int32)
    before = jnp.cumsum(onehot, axis=0) - onehot
    position = jnp.sum(before * onehot, axis=1)
    return flat * capacity + position


def dispatch(normed, slots, total_slots):
    table = (jnp.arange(total_slots, dtype=jnp.int32)[:, None] == slots[None, :]).astype(
        jnp.bfloat16
    )
    table = jnp.sum(table.reshape(total_slots, normed.shape[0], 2), axis=-1)
    return jnp.dot(table, normed, preferred_element_type=jnp.float32).astype(jnp.bfloat16)


def body(tokens, routes, combine, w_gate, w_up, w_down):
    tok_rows, width = tokens.shape
    exp_local = w_gate.shape[0]
    groups = lax.axis_size("exp")
    replicas = lax.axis_size("rep")
    experts = exp_local * groups
    capacity = max(2, 3 * tok_rows // experts)
    slots_per = exp_local * capacity
    normed = rms_rows(tokens)
    slots = slot_numbers(routes, experts, capacity)
    own = dispatch(normed, slots, experts * capacity).reshape(groups, slots_per, width)
    received = lax.all_to_all(own, "exp", split_axis=0, concat_axis=0, tiled=True)
    piece = lax.all_gather(received, "rep", axis=0, tiled=True)
    count = piece.shape[0]
    rows = piece.reshape(count, exp_local, capacity, width)
    gate = jnp.einsum("pkcd,kdf->pkcf", rows, w_gate, preferred_element_type=jnp.float32)
    up = jnp.einsum("pkcd,kdf->pkcf", rows, w_up, preferred_element_type=jnp.float32)
    hidden = (jax.nn.silu(gate) * up).astype(jnp.bfloat16)
    hidden = hidden.reshape(count, slots_per, hidden.shape[-1])
    rows = hidden.reshape(replicas * groups, exp_local, capacity, hidden.shape[-1])
    partial_terms = jnp.einsum("pkcf,kfd->pkcd", rows, w_down, preferred_element_type=jnp.float32)
    partial_terms = partial_terms.astype(jnp.bfloat16).reshape(replicas, groups, slots_per, width)
    arrived = lax.all_to_all(partial_terms, "rep", split_axis=0, concat_axis=0, tiled=True)
    summed = jnp.sum(arrived.astype(jnp.float32), axis=0)
    back = lax.all_to_all(
        summed.astype(jnp.bfloat16), "exp", split_axis=0, concat_axis=0, tiled=True
    )
    back = back.reshape(experts * capacity, width)
    picked = jnp.take(back, slots, axis=0).reshape(tok_rows, 2, width)
    mixed = jnp.sum(combine[:, :, None] * picked.astype(jnp.float32), axis=1)
    return mixed.astype(jnp.bfloat16)


def solution(mesh):
    in_specs = (
        P(("grp", "exp", "rep"), None),
        P(("grp", "exp", "rep"), None),
        P(("grp", "exp", "rep"), None),
        P("exp", None, "rep"),
        P("exp", None, "rep"),
        P("exp", "rep", None),
    )
    out_specs = P(("grp", "exp", "rep"), None)
    return jax.shard_map(body, mesh=mesh, in_specs=in_specs, out_specs=out_specs, check_vma=False)
```

profile of v0, /device:TPU:0, one launch (start us, length us, event | category | flops | bytes accessed | tf_op | source)
XLA Modules:
  0.0 162.4 jit_solution(15614619979951808762)
XLA Ops:
  6.5 0.9 copy.32
  7.5 0.1 eq.40
  7.6 0.1 reshape.100
  7.8 0.6 reduce-window.6
  8.4 0.2 slice_reduce_fusion
  8.7 0.1 reduce_sum.56
  8.9 0.7 compare_and_fusion
  9.7 1.1 fusion.21
  10.8 1.4 convolution_convert_fusion
  12.2 26.3 %all_to_all.15 = bf16[4,96,1024]{2,1,0:T(8,128)(2,1)} all-to-all(bf16[4,96,1024]{2,1,0:T(8,128)(2,1)S(1)} %bitcast.57), channel_id=1, replica_groups=mesh['grp'=2,'exp'=4,'rep'=4] {'exp'}, dimensions={0} | all-to-all | bytes 1572864 | tf_op jit(solution)/shard_map/all_to_all | solution.py:40
  38.5 27.8 %all-gather.2.cloned.1.call-done = bf16[16,96,1024]{2,1,0:T(8,128)(2,1)} async-done(((bf16[4,96,1024]{2,1,0:T(8,128)(2,1)}), bf16[16,96,1024]{2,1,0:T(8,128)(2,1)}) %all-gather.2.cloned.1.call-update) | async-done | bytes 3145744 | tf_op jit(solution)/shard_map/all_gather | solution.py:41
  66.3 6.0 %fusion.4 = f32[2,16,48,512]{3,2,1,0:T(8,128)} fusion(bf16[16,2,48,1024]{3,2,1,0:T(8,128)(2,1)} %bitcast.60, bf16[2,1024,512]{2,1,0:T(8,128)(2,1)} %param.10), kind=kOutput, calls=%fused_computation.9 | convolution fusion | flops 1610612736 | bytes 8388608 | tf_op jit(solution)/shard_map/pkcd,kdf->pkcf/dot_general | solution.py:45
  72.3 8.9 %convert_bitcast_fusion = bf16[16,2,48,1024]{3,2,0,1:T(8,128)(2,1)} fusion(bf16[2,512,1024]{2,1,0:T(8,128)(2,1)S(1)} %copy-done, f32[2,16,48,512]{3,2,1,0:T(8,128)} %fusion.4, bf16[16,2,48,1024]{3,2,1,0:T(8,128)(2,1)} %bitcast.61, bf16[2,1024,512]{2,1,0:T(8,128)(2,1)} %param.9), kind=kOutput, calls=%fused_computation.8 | convolution fusion | flops 3227516928 | bytes 13631488 | tf_op jit(solution)/shard_map/pkcf,kfd->pkcd/dot_general | solution.py:49
  81.2 2.4 %copy.38 = bf16[16,2,48,1024]{3,2,1,0:T(8,128)(2,1)S(1)} copy(bf16[16,2,48,1024]{3,2,0,1:T(8,128)(2,1)} %convert_bitcast_fusion) | data formatting | bytes 6291456 | tf_op jit(solution)/shard_map/convert_element_type | solution.py:50
  83.6 40.3 %all_to_all.16 = bf16[4,4,96,1024]{3,2,1,0:T(8,128)(2,1)} all-to-all(bf16[4,4,96,1024]{3,2,1,0:T(8,128)(2,1)S(1)} %bitcast.56), channel_id=1, replica_groups=mesh['grp'=2,'exp'=4,'rep'=4] {'rep'}, dimensions={0} | all-to-all | bytes 6291456 | tf_op jit(solution)/shard_map/all_to_all | solution.py:51
  123.9 3.6 %reduce_sum.59 = bf16[4,96,1024]{2,1,0:T(8,128)(2,1)} reduce(bf16[4,4,96,1024]{3,2,1,0:T(8,128)(2,1)} %all_to_all.16, bf16[]{:T(256)} %constant.30.clone.1), dimensions={0}, to_apply=%region_5.6 | reduce | flops 1179648 | bytes 3932162 | tf_op jit(solution)/shard_map/reduce_sum | solution.py:52
  127.5 4.6 %all-to-all-start.2 = ((bf16[4,96,1024]{2,1,0:T(8,128)(2,1)}), bf16[4,96,1024]{2,1,0:T(8,128)(2,1)S(1)}, u32[]{:S(2)}, u32[]{:S(2)}) async-start(bf16[4,96,1024]{2,1,0:T(8,128)(2,1)} %reduce_sum.59), calls=%async_computation.2 | async-start | bytes 1572864 | tf_op jit(solution)/shard_map/all_to_all | solution.py:53
  132.1 0.1 copy.39
  132.2 0.1 mul.61
  132.3 0.1 copy.35
  132.6 19.2 %all-to-all-done.2 = bf16[4,96,1024]{2,1,0:T(8,128)(2,1)S(1)} async-done(((bf16[4,96,1024]{2,1,0:T(8,128)(2,1)}), bf16[4,96,1024]{2,1,0:T(8,128)(2,1)S(1)}, u32[]{:S(2)}, u32[]{:S(2)}) %all-to-all-start.2) | async-done | bytes 786464 | tf_op jit(solution)/shard_map/all_to_all | solution.py:53
  151.8 1.2 gather_fusion
  153.0 0.2 gather.7
  153.2 2.4 %multiply_reduce_fusion = bf16[128,1024]{1,0:T(8,128)(2,1)} fusion(bf16[128,2,1024]{2,1,0:T(2,128)(2,1)S(1)} %gather.7, pred[128,2]{1,0:T(8,128)(4,1)S(1)} %copy.35, f32[128,2]{1,0:T(8,128)S(1)} %copy.31), kind=kLoop, calls=%fused_computation.18 | loop fusion | flops 917504 | bytes 787712 | tf_op jit(solution)/shard_map/reduce_sum | solution.py:58
  (19 shorter events, 0.4 us)
Async XLA Ops:
  6.5 65.8 %copy-start = (bf16[2,512,1024]{2,1,0:T(8,128)(2,1)S(1)}, bf16[2,512,1024]{2,1,0:T(8,128)(2,1)}, u32[]{:S(2)}) copy-start(bf16[2,512,1024]{2,1,0:T(8,128)(2,1)} %param.11) | copy-start | bytes 6291460
  6.5 59.8 %all-gather.2.cloned.1.call-start = ((), (), s32[]{:S(2)}) async-start(), calls=%async_computation.3 | async-start | bytes 3932160 | tf_op jit(solution)/shard_map/all_gather | solution.py:41
  123.9 8.2 %copy-start.1 = (s32[128,2]{0,1:T(2,128)S(1)}, s32[128,2]{0,1:T(2,128)}, u32[]{:S(2)}) copy-start(s32[128,2]{0,1:T(2,128)} %param.7) | copy-start | bytes 3076
  123.9 8.6 %copy-start.2 = (f32[128,2]{0,1:T(2,128)S(1)}, f32[128,2]{0,1:T(2,128)}, u32[]{:S(2)}) copy-start(f32[128,2]{0,1:T(2,128)} %param.8) | copy-start | bytes 3076
  127.5 24.3 %all-to-all-start.2 = ((bf16[4,96,1024]{2,1,0:T(8,128)(2,1)}), bf16[4,96,1024]{2,1,0:T(8,128)(2,1)S(1)}, u32[]{:S(2)}, u32[]{:S(2)}) async-start(bf16[4,96,1024]{2,1,0:T(8,128)(2,1)} %reduce_sum.59), calls=%async_computation.2 | async-start | bytes 1572864 | tf_op jit(solution)/shard_map/all_to_all | solution.py:53
Sparse Core Ops, SparseCore 0:
  38.6 27.6 all-gather.1
where the time goes:
time: 163 us; the launch traced here: 162 us
  blocking collectives  66.6 us (41%)
  waiting for transfers between devices  47 us (29%)
  matrix products  16.3 us (10%)
  between operations  13.5 us (8%)
  other arithmetic  8.59 us (5%)
  local copies, waits for them, and re-layouts  5.88 us (4%)
  starting transfers between devices  4.58 us (3%)
    all_to_all x1, blocking collectives, body(): lax.all_to_all(partial_terms, 'rep', split_axis=0, concat_axis=0, tiled=T...  40.3 us
    all_gather x1, waiting for transfers between devices, body(): piece = lax.all_gather(received, 'rep', axis=0, tiled=True)  27.8 us
    all_to_all x1, blocking collectives, body(): lax.all_to_all(own, 'exp', split_axis=0, concat_axis=0, tiled=True)  26.3 us
    all_to_all x1, waiting for transfers between devices, body(): lax.all_to_all(summed.astype(jnp.bfloat16), 'exp', split_axis=0, concat_a...  19.2 us
    dot_general x1, matrix products, body(): jnp.einsum('pkcf,kfd->pkcd', rows, w_down, preferred_element_type=jnp.flo...  8.89 us
    dot_general x1, matrix products, body(): jnp.einsum('pkcd,kdf->pkcf', rows, w_up, preferred_element_type=jnp.float32)  6.03 us
    all_to_all x1, starting transfers between devices, body(): lax.all_to_all(summed.astype(jnp.bfloat16), 'exp', split_axis=0, concat_a...  4.58 us
    reduce_sum x1, other arithmetic, body(): summed = jnp.sum(arrived.astype(jnp.float32), axis=0)  3.63 us
  transfers between devices with their start and end apart: 2, of which 2 were waited for; matrix products, arithmetic and copies ran while one was open for 0% of the time, Pallas kernels for 0%

commit v1 on v0

v1 whole, which is shorter than its diff:
```python
import functools

import jax
import jax.numpy as jnp
from jax import lax
from jax.experimental import pallas as pl
from jax.experimental.pallas import tpu as pltpu
from jax.sharding import PartitionSpec as P

MESH = pl.DeviceIdType.MESH
BF = jnp.bfloat16
F32 = jnp.float32


def kernel(
    K, n, X, cap, S,
    tok_ref, routes_ref, combine_ref, wg_hbm, wu_hbm, wd_hbm, out_ref,
    wg, wu, wd, own, rows, ckeep, csend, crecv, xkeep, xsend, xrecv, zsend, back, picks,
    w_sem, z_s, z_r, x_s, x_r, c_s, c_r, rc_s, rc_r, rx_s, rx_r, rz_s, rz_r,
):
    T = K * n
    D = tok_ref.shape[1]
    tok_rows = tok_ref.shape[0]
    z = lax.axis_index("exp")
    r = lax.axis_index("rep")
    x, c = r // 2, r % 2

    def at_z(o):
        return {"exp": (z + o + n) % n}

    def at_x(o):
        return {"rep": ((x + o + X) % X) * 2 + c}

    sibling = {"rep": x * 2 + 1 - c}

    def remote(src, dst, send, recv, where):
        return pltpu.make_async_remote_copy(
            src_ref=src, dst_ref=dst, send_sem=send, recv_sem=recv,
            device_id=where, device_id_type=MESH,
        )

    def z_copy(t, i):
        return remote(own.at[t], rows.at[t, 0, 0], z_s.at[t], z_r.at[t], at_z(-i))

    def x_copy(t, o):
        return remote(rows.at[t, 0, 0], rows.at[t, o, 0], x_s.at[t, o - 1], x_r.at[t, o - 1], at_x(-o))

    def c_copy(t, o):
        return remote(rows.at[t, o, 0], rows.at[t, o, 1], c_s.at[t, o], c_r.at[t, o], sibling)

    def rc_copy(t):
        return remote(csend.at[t], crecv.at[t], rc_s.at[t], rc_r.at[t], sibling)

    def rx_copy(t, o):
        return remote(xsend.at[t, o - 1], xrecv.at[t, o - 1], rx_s.at[t, o - 1], rx_r.at[t, o - 1], at_x(o))

    def rz_copy(t, i):
        return remote(zsend.at[t], back.at[t], rz_s.at[t], rz_r.at[t], at_z(i))

    def w_copies(k):
        return [
            pltpu.make_async_copy(src.at[k], dst.at[k], w_sem.at[m, k])
            for m, (src, dst) in enumerate(((wg_hbm, wg), (wu_hbm, wu), (wd_hbm, wd)))
        ]

    barrier = pltpu.get_barrier_semaphore()
    for o in range(1, n):
        pl.semaphore_signal(barrier, inc=1, device_id=at_z(o), device_id_type=MESH)
    for o in range(1, X):
        pl.semaphore_signal(barrier, inc=1, device_id=at_x(o), device_id_type=MESH)
    pl.semaphore_signal(barrier, inc=1, device_id=sibling, device_id_type=MESH)

    for k in range(K):
        for copy in w_copies(k):
            copy.start()

    values = tok_ref[...].astype(F32)
    scale = lax.rsqrt(jnp.mean(values * values, axis=-1, keepdims=True) + 1e-05)
    normed = (values * scale).astype(BF)
    experts = n * K
    lanes = max(128, experts)
    expert_ids = lax.broadcasted_iota(jnp.int32, (tok_rows, lanes), 1)
    hot = [(routes_ref[:, j : j + 1] == expert_ids).astype(F32) for j in range(2)]
    tri = (
        lax.broadcasted_iota(jnp.int32, (tok_rows, tok_rows), 1)
        < lax.broadcasted_iota(jnp.int32, (tok_rows, tok_rows), 0)
    ).astype(F32).astype(BF)
    before = jnp.dot(tri, (hot[0] + hot[1]).astype(BF), preferred_element_type=F32)
    slot_ids = lax.broadcasted_iota(jnp.int32, (tok_rows, T * S), 1)
    table = []
    for j in range(2):
        position = jnp.sum(before * hot[j], axis=1, keepdims=True).astype(jnp.int32)
        e = routes_ref[:, j : j + 1]
        ze = lax.div(e, jnp.full_like(e, K))
        ke = e - ze * K
        ie = z - ze
        ie = jnp.where(ie < 0, ie + n, ie)
        slot = (ke * n + ie) * S + position
        table.append((slot == slot_ids).astype(F32))
        picks[j] = table[j].astype(BF)
    sent = lax.dot_general(
        (table[0] + table[1]).astype(BF), normed, (((0,), (0,)), ((), ())), preferred_element_type=F32
    ).astype(BF).reshape(T, S, D)
    own[...] = sent
    for k in range(K):
        rows[k * n, 0, 0] = sent[k * n]

    pl.semaphore_wait(barrier, n + X - 1)
    for k in range(K):
        @pl.loop(1, n)
        def _(i):
            z_copy(k * n + i, i).start()

    def stage_a(t):
        i = t % n

        @pl.when(i > 0)
        def _():
            z_copy(t, i).wait_recv()

        for o in range(1, X):
            x_copy(t, o).start()
        c_copy(t, 0).start()

    def stage_b(t):
        for o in range(1, X):
            x_copy(t, o).wait_recv()
            c_copy(t, o).start()

    def stage_c(t):
        k = t // n

        @pl.when(t % n == 0)
        def _():
            for copy in w_copies(k):
                copy.wait()

        for o in range(X):
            c_copy(t, o).wait_recv()
        a = rows[t].reshape(X * 2 * S, D)
        gate = jnp.dot(a, wg[k], preferred_element_type=F32)
        up = jnp.dot(a, wu[k], preferred_element_type=F32)
        hidden = (gate / (1.0 + jnp.exp(-gate)) * up).astype(BF)
        part = jnp.dot(hidden, wd[k], preferred_element_type=F32).reshape(X, 2, S, D)
        csend[t] = part[:, 1].astype(BF)
        rc_copy(t).start()
        ckeep[t % 2] = part[:, 0]

    def stage_d(t):
        rc_copy(t).wait_recv()
        for o in range(1, X):
            xsend[t, o - 1] = (ckeep[t % 2, o] + crecv[t, o].astype(F32)).astype(BF)
            rx_copy(t, o).start()
        xkeep[t % 2] = ckeep[t % 2, 0] + crecv[t, 0].astype(F32)

    def stage_e(t):
        i = t % n
        total = xkeep[t % 2]
        for o in range(1, X):
            rx_copy(t, o).wait_recv()
            total = total + xrecv[t, o - 1].astype(F32)
        total = total.astype(BF)

        @pl.when(i > 0)
        def _():
            zsend[t] = total
            rz_copy(t, i).start()

        @pl.when(i == 0)
        def _():
            back[t] = total

    stages = ((0, stage_a), (1, stage_b), (4, stage_e), (3, stage_d), (2, stage_c))

    @pl.loop(0, T + 4)
    def _(tick):
        for lag, stage in stages:
            @pl.when((tick >= lag) & (tick < T + lag))
            def _(lag=lag, stage=stage):
                stage(tick - lag)

    for k in range(K):
        @pl.loop(1, n)
        def _(i):
            rz_copy(k * n + i, i).wait_recv()

    landed = back[...].reshape(T * S, D)
    mixed = combine_ref[:, 0:1] * jnp.dot(picks[0], landed, preferred_element_type=F32)
    mixed = mixed + combine_ref[:, 1:2] * jnp.dot(picks[1], landed, preferred_element_type=F32)
    out_ref[...] = mixed.astype(BF)

    @pl.loop(0, T)
    def _(t):
        i = t % n

        @pl.when(i > 0)
        def _():
            z_copy(t, i).wait_send()
            rz_copy(t, i).wait_send()

        for o in range(X):
            c_copy(t, o).wait_send()
        rc_copy(t).wait_send()
        for o in range(1, X):
            x_copy(t, o).wait_send()
            rx_copy(t, o).wait_send()


def body(n, R, tokens, routes, combine, w_gate, w_up, w_down):
    tok_rows, D = tokens.shape
    K, _, F = w_gate.shape
    X = R // 2
    cap = max(2, 3 * tok_rows // (K * n))
    S = -(-cap // 16) * 16
    T = K * n
    vmem = pl.BlockSpec(memory_space=pltpu.VMEM)
    hbm = pl.BlockSpec(memory_space=pl.ANY)
    dma = pltpu.SemaphoreType.DMA
    macs = T * X * 2 * S * D * F * 3
    return pl.pallas_call(
        functools.partial(kernel, K, n, X, cap, S),
        out_shape=jax.ShapeDtypeStruct((tok_rows, D), BF),
        in_specs=[vmem, vmem, vmem, hbm, hbm, hbm],
        out_specs=vmem,
        scratch_shapes=[
            pltpu.VMEM((K, D, F), BF),
            pltpu.VMEM((K, D, F), BF),
            pltpu.VMEM((K, F, D), BF),
            pltpu.VMEM((T, S, D), BF),
            pltpu.VMEM((T, X, 2, S, D), BF),
            pltpu.VMEM((2, X, S, D), F32),
            pltpu.VMEM((T, X, S, D), BF),
            pltpu.VMEM((T, X, S, D), BF),
            pltpu.VMEM((2, S, D), F32),
            pltpu.VMEM((T, X - 1, S, D), BF),
            pltpu.VMEM((T, X - 1, S, D), BF),
            pltpu.VMEM((T, S, D), BF),
            pltpu.VMEM((T, S, D), BF),
            pltpu.VMEM((2, tok_rows, T * S), BF),
            dma((3, K)),
            dma((T,)), dma((T,)),
            dma((T, X - 1)), dma((T, X - 1)),
            dma((T, X)), dma((T, X)),
            dma((T,)), dma((T,)),
            dma((T, X - 1)), dma((T, X - 1)),
            dma((T,)), dma((T,)),
        ],
        compiler_params=pltpu.CompilerParams(
            collective_id=0, has_side_effects=True, vmem_limit_bytes=60 * 1024 * 1024
        ),
        cost_estimate=pl.CostEstimate(flops=2 * macs, bytes_accessed=6 * K * D * F, transcendentals=T * X * 2 * S * F),
    )(tokens, routes, combine, w_gate, w_up, w_down)


def solution(mesh):
    in_specs = (
        P(("grp", "exp", "rep"), None),
        P(("grp", "exp", "rep"), None),
        P(("grp", "exp", "rep"), None),
        P("exp", None, "rep"),
        P("exp", None, "rep"),
        P("exp", "rep", None),
    )
    out_specs = P(("grp", "exp", "rep"), None)
    return jax.shard_map(
        functools.partial(body, mesh.shape["exp"], mesh.shape["rep"]),
        mesh=mesh, in_specs=in_specs, out_specs=out_specs, check_vma=False,
    )
```

time: 163 us -> 65.1 us (0.40)
  blocking collectives: 66.6 us -> 0 us
  Pallas kernels: 0 us -> 60.4 us
  waiting for transfers between devices: 47 us -> 0 us
  matrix products: 16.3 us -> 0 us
  between operations: 13.5 us -> 0.01 us
  other arithmetic: 8.59 us -> 0 us
  starting transfers between devices: 4.58 us -> 0 us
    all_to_all x2 -> x0, blocking collectives: 66.6 us -> none  [the longest x1 40.3 us: body(): lax.all_to_all(partial_terms, 'rep', split_axis=0, concat_axis=0, tiled=T...]
    pallas_call x0 -> x1, Pallas kernels: none -> 60.4 us  [body(): pl.pallas_call(functools.partial(kernel, K, n, X, cap, S), out_shape=jax....]
    all_gather x1 -> x0, waiting for transfers between devices: 27.8 us -> none  [body(): piece = lax.all_gather(received, 'rep', axis=0, tiled=True)]
    all_to_all x1 -> x0, waiting for transfers between devices: 19.2 us -> none  [body(): lax.all_to_all(summed.astype(jnp.bfloat16), 'exp', split_axis=0, concat_a...]
    dot_general x3 -> x0, matrix products: 16.3 us -> none  [the longest x1 8.89 us: body(): jnp.einsum('pkcf,kfd->pkcd', rows, w_down, preferred_element_type=jnp.flo...]
    reduce_sum x5 -> x0, other arithmetic: 7.22 us -> none  [the longest x1 3.63 us: body(): summed = jnp.sum(arrived.astype(jnp.float32), axis=0)]
    all_to_all x1 -> x0, starting transfers between devices: 4.58 us -> none  [body(): lax.all_to_all(summed.astype(jnp.bfloat16), 'exp', split_axis=0, concat_a...]
    unnamed x8 -> x3, local copies, waits for them, and re-layouts: 1.06 us -> 4.48 us
  transfers between devices with their start and end apart: 2 -> 0, of which waited for: 2 -> 0; matrix products, arithmetic and copies ran while one was open for 0% -> 0% of each run, Pallas kernels for 0% -> 0%
where the time goes in v1:
time: 65.1 us; the launch traced here: 64.9 us
  Pallas kernels  60.4 us (93%)
  local copies, waits for them, and re-layouts  4.48 us (7%)
    pallas_call x1, Pallas kernels, body(): pl.pallas_call(functools.partial(kernel, K, n, X, cap, S), out_shape=jax....  60.4 us
    unnamed x3, local copies, waits for them, and re-layouts  4.48 us

profile of v1, /device:TPU:0, one launch (start us, length us, event | category | flops | bytes accessed | tf_op | source)
XLA Modules:
  0.0 64.9 jit_solution(12800243273188704858)
XLA Ops:
  0.0 1.4 %copy.7.routes_ref = s32[128,2]{1,0:T(8,128)} copy(s32[128,2]{0,1:T(2,128)} %param.7) | data formatting | bytes 2048 | tf_op args[1]
  1.4 1.4 %copy.8.combine_ref = f32[128,2]{1,0:T(8,128)} copy(f32[128,2]{0,1:T(2,128)} %param.8) | data formatting | bytes 2048 | tf_op args[2]
  2.8 60.4 %shard_map.64 = bf16[128,1024]{1,0:T(8,128)(2,1)} custom-call(bf16[128,1024]{1,0:T(8,128)(2,1)} %tok_ref.1, s32[128,2]{1,0:T(8,128)} %copy.7.routes_ref, f32[128,2]{1,0:T(8,128)} %copy.8.combine_ref, bf16[2,1024,512]{2,1,0:T(8,128)(2,1)} %wg_hbm.1, bf16[2,1024,512]{2,1,0:T(8,128)(2,1)} %wu_hbm.1, bf16[2,512,1024]{2,1,0:T(8,128)(2,1)} %wd_hbm.1), custom_call_target="tpu_custom_call" | custom-call | flops 4831838208 | bytes 6291456 | tf_op jit(solution)/shard_map/pallas_call | solution.py:220
  63.2 1.7 %copy.10 = bf16[128,1024]{1,0:T(8,128)(2,1)} copy(bf16[128,1024]{1,0:T(8,128)(2,1)} %shard_map.64) | data formatting | bytes 524288

commit v2 on v1

--- a/solution.py
+++ b/solution.py
@@ -10,6 +10,8 @@
 MESH = pl.DeviceIdType.MESH
 BF = jnp.bfloat16
 F32 = jnp.float32
+WINDOW = 2
+LAGS = (0, 1, 2, 3, 5)
 
 
 def kernel(
@@ -39,6 +41,10 @@
             device_id=where, device_id_type=MESH,
         )
 
+    def tile(t):
+        k = t // n
+        return k, jnp.where(k == K - 1, t % n + 1, t % n) % n
+
     def z_copy(t, i):
         return remote(own.at[t], rows.at[t, 0, 0], z_s.at[t], z_r.at[t], at_z(-i))
 
@@ -73,6 +79,7 @@
     for k in range(K):
         for copy in w_copies(k):
             copy.start()
+    routes = jnp.transpose(jnp.concatenate([routes_ref[...]] * 4, axis=0))
 
     values = tok_ref[...].astype(F32)
     scale = lax.rsqrt(jnp.mean(values * values, axis=-1, keepdims=True) + 1e-05)
@@ -80,7 +87,7 @@
     experts = n * K
     lanes = max(128, experts)
     expert_ids = lax.broadcasted_iota(jnp.int32, (tok_rows, lanes), 1)
-    hot = [(routes_ref[:, j : j + 1] == expert_ids).astype(F32) for j in range(2)]
+    hot = [(routes[:, j : j + 1] == expert_ids).astype(F32) for j in range(2)]
     tri = (
         lax.broadcasted_iota(jnp.int32, (tok_rows, tok_rows), 1)
         < lax.broadcasted_iota(jnp.int32, (tok_rows, tok_rows), 0)
@@ -90,11 +97,12 @@
     table = []
     for j in range(2):
         position = jnp.sum(before * hot[j], axis=1, keepdims=True).astype(jnp.int32)
-        e = routes_ref[:, j : j + 1]
+        e = routes[:, j : j + 1]
         ze = lax.div(e, jnp.full_like(e, K))
         ke = e - ze * K
         ie = z - ze
         ie = jnp.where(ie < 0, ie + n, ie)
+        ie = jnp.where(ke == K - 1, jnp.where(ie == 0, n - 1, ie - 1), ie)
         slot = (ke * n + ie) * S + position
         table.append((slot == slot_ids).astype(F32))
         picks[j] = table[j].astype(BF)
@@ -102,26 +110,39 @@
         (table[0] + table[1]).astype(BF), normed, (((0,), (0,)), ((), ())), preferred_element_type=F32
     ).astype(BF).reshape(T, S, D)
     own[...] = sent
-    for k in range(K):
-        rows[k * n, 0, 0] = sent[k * n]
+    own_tiles = [k * n for k in range(K - 1)] + [T - 1]
+    for t in own_tiles:
+        rows[t, 0, 0] = sent[t]
+
+    def send_z(t):
+        i = tile(t)[1]
+
+        @pl.when(i > 0)
+        def _():
+            z_copy(t, i).start()
 
     pl.semaphore_wait(barrier, n + X - 1)
-    for k in range(K):
-        @pl.loop(1, n)
-        def _(i):
-            z_copy(k * n + i, i).start()
-
-    def stage_a(t):
-        i = t % n
-
-        @pl.when(i > 0)
-        def _():
-            z_copy(t, i).wait_recv()
-
+    for t in range(min(WINDOW, T)):
+        send_z(jnp.int32(t))
+    for t in own_tiles:
         for o in range(1, X):
             x_copy(t, o).start()
         c_copy(t, 0).start()
 
+    def stage_a(t):
+        i = tile(t)[1]
+
+        @pl.when(i > 0)
+        def _():
+            z_copy(t, i).wait_recv()
+            for o in range(1, X):
+                x_copy(t, o).start()
+            c_copy(t, 0).start()
+
+        @pl.when(t + WINDOW < T)
+        def _():
+            send_z(t + WINDOW)
+
     def stage_b(t):
         for o in range(1, X):
             x_copy(t, o).wait_recv()
@@ -130,7 +151,7 @@
     def stage_c(t):
         k = t // n
 
-        @pl.when(t % n == 0)
+        @pl.when(t == k * n)
         def _():
             for copy in w_copies(k):
                 copy.wait()
@@ -144,18 +165,18 @@
         part = jnp.dot(hidden, wd[k], preferred_element_type=F32).reshape(X, 2, S, D)
         csend[t] = part[:, 1].astype(BF)
         rc_copy(t).start()
-        ckeep[t % 2] = part[:, 0]
+        ckeep[t % 4] = part[:, 0]
 
     def stage_d(t):
         rc_copy(t).wait_recv()
         for o in range(1, X):
-            xsend[t, o - 1] = (ckeep[t % 2, o] + crecv[t, o].astype(F32)).astype(BF)
+            xsend[t, o - 1] = (ckeep[t % 4, o] + crecv[t, o].astype(F32)).astype(BF)
             rx_copy(t, o).start()
-        xkeep[t % 2] = ckeep[t % 2, 0] + crecv[t, 0].astype(F32)
+        xkeep[t % 4] = ckeep[t % 4, 0] + crecv[t, 0].astype(F32)
 
     def stage_e(t):
-        i = t % n
-        total = xkeep[t % 2]
+        i = tile(t)[1]
+        total = xkeep[t % 4]
         for o in range(1, X):
             rx_copy(t, o).wait_recv()
             total = total + xrecv[t, o - 1].astype(F32)
@@ -170,28 +191,33 @@
         def _():
             back[t] = total
 
-    stages = ((0, stage_a), (1, stage_b), (4, stage_e), (3, stage_d), (2, stage_c))
-
-    @pl.loop(0, T + 4)
+    lag = LAGS
+    stages = ((lag[0], stage_a), (lag[4], stage_e), (lag[3], stage_d), (lag[1], stage_b), (lag[2], stage_c))
+
+    @pl.loop(0, T + max(LAGS))
     def _(tick):
         for lag, stage in stages:
             @pl.when((tick >= lag) & (tick < T + lag))
             def _(lag=lag, stage=stage):
                 stage(tick - lag)
 
-    for k in range(K):
-        @pl.loop(1, n)
-        def _(i):
-            rz_copy(k * n + i, i).wait_recv()
-
-    landed = back[...].reshape(T * S, D)
-    mixed = combine_ref[:, 0:1] * jnp.dot(picks[0], landed, preferred_element_type=F32)
-    mixed = mixed + combine_ref[:, 1:2] * jnp.dot(picks[1], landed, preferred_element_type=F32)
-    out_ref[...] = mixed.astype(BF)
-
     @pl.loop(0, T)
     def _(t):
-        i = t % n
+        i = tile(t)[1]
+
+        @pl.when(i > 0)
+        def _():
+            rz_copy(t, i).wait_recv()
+
+    landed = back[...].reshape(T * S, D)
+    combine = jnp.transpose(jnp.concatenate([combine_ref[...]] * 4, axis=0))
+    mixed = combine[:, 0:1] * jnp.dot(picks[0], landed, preferred_element_type=F32)
+    mixed = mixed + combine[:, 1:2] * jnp.dot(picks[1], landed, preferred_element_type=F32)
+    out_ref[...] = mixed.astype(BF)
+
+    @pl.loop(0, T)
+    def _(t):
+        i = tile(t)[1]
 
         @pl.when(i > 0)
         def _():
@@ -228,10 +254,10 @@
             pltpu.VMEM((K, F, D), BF),
             pltpu.VMEM((T, S, D), BF),
             pltpu.VMEM((T, X, 2, S, D), BF),
-            pltpu.VMEM((2, X, S, D), F32),
+            pltpu.VMEM((4, X, S, D), F32),
             pltpu.VMEM((T, X, S, D), BF),
             pltpu.VMEM((T, X, S, D), BF),
-            pltpu.VMEM((2, S, D), F32),
+            pltpu.VMEM((4, S, D), F32),
             pltpu.VMEM((T, X - 1, S, D), BF),
             pltpu.VMEM((T, X - 1, S, D), BF),
             pltpu.VMEM((T, S, D), BF),
@@ -249,7 +275,7 @@
             collective_id=0, has_side_effects=True, vmem_limit_bytes=60 * 1024 * 1024
         ),
         cost_estimate=pl.CostEstimate(flops=2 * macs, bytes_accessed=6 * K * D * F, transcendentals=T * X * 2 * S * F),
-    )(tokens, routes, combine, w_gate, w_up, w_down)
+    )(tokens, routes.T, combine.T, w_gate, w_up, w_down)
 
 
 def solution(mesh):

time: 65.1 us -> 53.2 us (0.82)
  Pallas kernels: 60.4 us -> 51.4 us
  local copies, waits for them, and re-layouts: 4.48 us -> 1.67 us
    pallas_call x1, Pallas kernels: 60.4 us -> 51.4 us  [body(): pl.pallas_call(functools.partial(kernel, K, n, X, cap, S), out_shape=jax....]
    unnamed x3 -> x1, local copies, waits for them, and re-layouts: 4.48 us -> 1.67 us
where the time goes in v2:
time: 53.2 us; the launch traced here: 53.1 us
  Pallas kernels  51.4 us (97%)
  local copies, waits for them, and re-layouts  1.67 us (3%)
    pallas_call x1, Pallas kernels, body(): pl.pallas_call(functools.partial(kernel, K, n, X, cap, S), out_shape=jax....  51.4 us
    unnamed x1, local copies, waits for them, and re-layouts  1.67 us

profile of v2, /device:TPU:0, one launch (start us, length us, event | category | flops | bytes accessed | tf_op | source)
XLA Modules:
  0.0 53.1 jit_solution(16672101876049509252)
XLA Ops:
  0.0 51.4 %shard_map.64 = bf16[128,1024]{1,0:T(8,128)(2,1)} custom-call(bf16[128,1024]{1,0:T(8,128)(2,1)} %tok_ref.1, s32[2,128]{1,0:T(2,128)} %bitcast.2, f32[2,128]{1,0:T(2,128)} %bitcast.3, bf16[2,1024,512]{2,1,0:T(8,128)(2,1)} %wg_hbm.1, bf16[2,1024,512]{2,1,0:T(8,128)(2,1)} %wu_hbm.1, bf16[2,512,1024]{2,1,0:T(8,128)(2,1)} %wd_hbm.1), custom_call_target="tpu_custom_call" | custom-call | flops 4831838208 | bytes 6291456 | tf_op jit(solution)/shard_map/pallas_call | solution.py:246
  51.4 1.7 %copy.8 = bf16[128,1024]{1,0:T(8,128)(2,1)} copy(bf16[128,1024]{1,0:T(8,128)(2,1)} %shard_map.64) | data formatting | bytes 524288

commit v3 on v2

--- a/solution.py
+++ b/solution.py
@@ -11,7 +11,7 @@
 BF = jnp.bfloat16
 F32 = jnp.float32
 WINDOW = 2
-LAGS = (0, 1, 2, 3, 5)
+LAGS = (0, 2, 3, 4, 6)
 
 
 def kernel(
@@ -191,13 +191,18 @@
         def _():
             back[t] = total
 
+    stage_a(0)
+    stage_b(0)
+    stage_c(0)
+    stage_a(1)
+    stage_d(0)
     lag = LAGS
-    stages = ((lag[0], stage_a), (lag[4], stage_e), (lag[3], stage_d), (lag[1], stage_b), (lag[2], stage_c))
-
-    @pl.loop(0, T + max(LAGS))
+    stages = ((lag[0], 2, stage_a), (lag[4], 0, stage_e), (lag[3], 1, stage_d), (lag[1], 1, stage_b), (lag[2], 1, stage_c))
+
+    @pl.loop(2, T + max(LAGS))
     def _(tick):
-        for lag, stage in stages:
-            @pl.when((tick >= lag) & (tick < T + lag))
+        for lag, first, stage in stages:
+            @pl.when((tick >= lag + first) & (tick < T + lag))
             def _(lag=lag, stage=stage):
                 stage(tick - lag)
 

time: 53.2 us -> 51.7 us (0.972)
  Pallas kernels: 51.4 us -> 49.9 us
    pallas_call x1, Pallas kernels: 51.4 us -> 49.9 us  [body(): pl.pallas_call(functools.partial(kernel, K, n, X, cap, S), out_shape=jax....]
where the time goes in v3:
time: 51.7 us; the launch traced here: 51.6 us
  Pallas kernels  49.9 us (97%)
  local copies, waits for them, and re-layouts  1.67 us (3%)
    pallas_call x1, Pallas kernels, body(): pl.pallas_call(functools.partial(kernel, K, n, X, cap, S), out_shape=jax....  49.9 us
    unnamed x1, local copies, waits for them, and re-layouts  1.67 us

profile of v3, /device:TPU:0, one launch (start us, length us, event | category | flops | bytes accessed | tf_op | source)
XLA Modules:
  0.0 51.6 jit_solution(1668693767110147107)
XLA Ops:
  0.0 49.9 %shard_map.64 = bf16[128,1024]{1,0:T(8,128)(2,1)} custom-call(bf16[128,1024]{1,0:T(8,128)(2,1)} %tok_ref.1, s32[2,128]{1,0:T(2,128)} %bitcast.2, f32[2,128]{1,0:T(2,128)} %bitcast.3, bf16[2,1024,512]{2,1,0:T(8,128)(2,1)} %wg_hbm.1, bf16[2,1024,512]{2,1,0:T(8,128)(2,1)} %wu_hbm.1, bf16[2,512,1024]{2,1,0:T(8,128)(2,1)} %wd_hbm.1), custom_call_target="tpu_custom_call" | custom-call | flops 4831838208 | bytes 6291456 | tf_op jit(solution)/shard_map/pallas_call | solution.py:251
  49.9 1.7 %copy.8 = bf16[128,1024]{1,0:T(8,128)(2,1)} copy(bf16[128,1024]{1,0:T(8,128)(2,1)} %shard_map.64) | data formatting | bytes 524288

commit v4 on v3

--- a/solution.py
+++ b/solution.py
@@ -197,7 +197,7 @@
     stage_a(1)
     stage_d(0)
     lag = LAGS
-    stages = ((lag[0], 2, stage_a), (lag[4], 0, stage_e), (lag[3], 1, stage_d), (lag[1], 1, stage_b), (lag[2], 1, stage_c))
+    stages = ((lag[0], 2, stage_a), (lag[4], 0, stage_e), (lag[1], 1, stage_b), (lag[3], 1, stage_d), (lag[2], 1, stage_c))
 
     @pl.loop(2, T + max(LAGS))
     def _(tick):

time: 51.7 us -> 51.7 us (level)
  no operation moved by 1% of the time
where the time goes in v4:
time: 51.7 us; the launch traced here: 51.6 us
  Pallas kernels  49.9 us (97%)
  local copies, waits for them, and re-layouts  1.67 us (3%)
    pallas_call x1, Pallas kernels, body(): pl.pallas_call(functools.partial(kernel, K, n, X, cap, S), out_shape=jax....  49.9 us
    unnamed x1, local copies, waits for them, and re-layouts  1.67 us

profile of v4, /device:TPU:0, one launch (start us, length us, event | category | flops | bytes accessed | tf_op | source)
XLA Modules:
  0.0 51.6 jit_solution(12311936331666648696)
XLA Ops:
  0.0 49.9 %shard_map.64 = bf16[128,1024]{1,0:T(8,128)(2,1)} custom-call(bf16[128,1024]{1,0:T(8,128)(2,1)} %tok_ref.1, s32[2,128]{1,0:T(2,128)} %bitcast.2, f32[2,128]{1,0:T(2,128)} %bitcast.3, bf16[2,1024,512]{2,1,0:T(8,128)(2,1)} %wg_hbm.1, bf16[2,1024,512]{2,1,0:T(8,128)(2,1)} %wu_hbm.1, bf16[2,512,1024]{2,1,0:T(8,128)(2,1)} %wd_hbm.1), custom_call_target="tpu_custom_call" | custom-call | flops 4831838208 | bytes 6291456 | tf_op jit(solution)/shard_map/pallas_call | solution.py:251
  49.9 1.7 %copy.8 = bf16[128,1024]{1,0:T(8,128)(2,1)} copy(bf16[128,1024]{1,0:T(8,128)(2,1)} %shard_map.64) | data formatting | bytes 524288
